TPU v7x, 512 devices: a whole 4x8x8 slice. The times are simulated.
512 devices in a mesh: chan: 8 (over y_hi, core), dp: 64 (over z, x, y_lo).
Axes of the slice: x: 4, y: 8 (y_hi: 4, y_lo: 2; y = y_hi * 2 + y_lo), z: 8, core: 2. Of those that a mesh axis runs over, the one named last changes fastest.
Arguments:
- volume: bfloat16 [128, 32, 32, 256], P('dp', None, None, 'chan'), may hold values from -6 to 6
- filter_one: bfloat16 [3, 3, 3, 256, 256], P(None, None, None, 'chan'), may hold values from -0.078125 to 0.078125
- filter_two: bfloat16 [3, 3, 3, 256, 256], P(None, None, None, 'chan'), may hold values from -0.078125 to 0.078125
- cotangent: bfloat16 [128, 32, 32, 256], P('dp', None, None, 'chan'), may hold values from -6 to 6
Outputs:
- output: bfloat16 [128, 32, 32, 256], P('dp', None, None, 'chan')
- input_grad: bfloat16 [128, 32, 32, 256], P('dp', None, None, 'chan')
- grad_one: float32 [3, 3, 3, 256, 256], P(None, None, None, 'chan')
- grad_two: float32 [3, 3, 3, 256, 256], P(None, None, None, 'chan')
All inputs are finite; a program needn't handle non-finite values.
Results may differ from a plain program's by a relative error of at most 0.02525.
The roundings to bfloat16 on the way count: a program that leaves them out, or rounds other values in their place, can miss the bound.
Values may be sent and summed in bfloat16 or wider, within the bound.
A program may use at most 128 MiB of HBM per device.

v0:
```python
import math

import jax
import jax.numpy as jnp
from jax import lax
from jax.sharding import PartitionSpec as P

VOX = 32


SLOPE = 0.3


def extended(block, sides, width):
    for axis, dim in sides:
        count = lax.axis_size(axis)
        forward = [(i, i + 1) for i in range(count - 1)]
        forward.append((count - 1, 0))
        backward = [(target, source) for source, target in forward]
        low = lax.ppermute(
            lax.slice_in_dim(block, block.shape[dim] - width, None, axis=dim), axis, forward
        )
        high = lax.ppermute(lax.slice_in_dim(block, 0, width, axis=dim), axis, backward)
        block = jnp.concatenate([low, block, high], axis=dim)
    return block


def leaky(values):
    return jnp.where(values > 0, values, SLOPE * values)


def slope_of(values):
    return jnp.where(values > 0, jnp.float32(1.0), jnp.float32(SLOPE))


def tap_mask(rows, offset):
    base = lax.axis_index("dp") * rows
    total_rows = lax.axis_size("dp") * rows
    planes = jnp.mod(base + jnp.arange(rows, dtype=jnp.int32) - 1, total_rows)
    depth = jnp.mod(planes, VOX) + offset
    inside = jnp.logical_and(depth >= 0, depth < VOX)
    return inside[:, None, None, None]


def pad_plane(values):
    return jnp.pad(values, ((0, 0), (1, 1), (1, 1), (0, 0)))


def columns(plane, rows, height, breadth):
    taps = []
    for a in range(3):
        inside = tap_mask(rows, a - 1)
        depth_slab = plane[a : a + rows]
        depth_slab = jnp.where(inside, depth_slab, jnp.zeros_like(depth_slab))
        for b in range(3):
            for c in range(3):
                taps.append(depth_slab[:, b : b + height, c : c + breadth, :])
    stacked = jnp.concatenate(taps, axis=-1)
    return stacked.reshape(rows * height * breadth, stacked.shape[-1])


def local(volume, filter_one, filter_two, cotangent):
    rows, height, breadth, narrow = volume.shape
    full = filter_one.shape[4]
    voxels = rows * height * breadth
    scale = 1.0 / math.sqrt(lax.axis_size("dp") * voxels)

    def forward(activity, weight):
        rim = extended(activity, (("dp", 0),), 1)
        plane = pad_plane(rim)
        stacked = columns(plane, rows, height, breadth)
        partial_value = jnp.dot(
            stacked, weight.reshape(27 * narrow, full), preferred_element_type=jnp.float32
        )
        summed = lax.psum_scatter(partial_value, "chan", scatter_dimension=1, tiled=True)
        return (plane, summed)

    def backward(plane, delta, weight):
        wide = lax.all_gather(delta, "chan", axis=3, tiled=True)
        rim = extended(wide, (("dp", 0),), 1)
        centre = rim[1 : rows + 1].reshape(voxels, full)
        stacked = columns(plane, rows, height, breadth)
        weight_grad = lax.dot_general(
            stacked, centre, (((0,), (0,)), ((), ())), preferred_element_type=jnp.float32
        )
        weight_grad = weight_grad.reshape(3, 3, 3, narrow, full)
        source = pad_plane(rim)
        total = jnp.zeros((rows, height, breadth, narrow), jnp.float32)
        for a in range(3):
            depth_slab = source[2 - a : 2 - a + rows]
            flat = depth_slab.reshape(-1, full)
            product = lax.dot_general(
                flat,
                weight[a].reshape(9 * narrow, full),
                (((1,), (1,)), ((), ())),
                preferred_element_type=jnp.float32,
            )
            product = product.reshape(rows, height + 2, breadth + 2, 9, narrow)
            part = jnp.zeros((rows, height, breadth, narrow), jnp.float32)
            for b in range(3):
                for c in range(3):
                    part = (
                        part
                        + product[:, 2 - b : 2 - b + height, 2 - c : 2 - c + breadth, b * 3 + c, :]
                    )
            inside = tap_mask(rows, 1 - a)
            total = total + jnp.where(inside, part, jnp.zeros_like(part))
        return (weight_grad, total.reshape(voxels, narrow))

    def layer_sum(weight_grad):
        return lax.psum(weight_grad, "dp")

    plane_one, pre_one = forward(volume, filter_one)
    act_one = leaky(pre_one).astype(jnp.bfloat16).reshape(rows, height, breadth, narrow)
    plane_two, pre_two = forward(act_one, filter_two)
    output = leaky(pre_two).astype(jnp.bfloat16).reshape(rows, height, breadth, narrow)
    delta_two = (cotangent.reshape(voxels, narrow).astype(jnp.float32) * slope_of(pre_two)).astype(
        jnp.bfloat16
    )
    local_two, back_two = backward(
        plane_two, delta_two.reshape(rows, height, breadth, narrow), filter_two
    )
    summed_two = layer_sum(local_two)
    delta_one = (back_two * slope_of(pre_one)).astype(jnp.bfloat16)
    local_one, back_one = backward(
        plane_one, delta_one.reshape(rows, height, breadth, narrow), filter_one
    )
    summed_one = layer_sum(local_one)
    input_grad = back_one.astype(jnp.bfloat16).reshape(rows, height, breadth, narrow)
    return (output, input_grad, summed_one * scale, summed_two * scale)


def solution(mesh):
    in_specs = (
        P("dp", None, None, "chan"),
        P(None, None, None, "chan", None),
        P(None, None, None, "chan", None),
        P("dp", None, None, "chan"),
    )
    out_specs = (
        P("dp", None, None, "chan"),
        P("dp", None, None, "chan"),
        P(None, None, None, "chan", None),
        P(None, None, None, "chan", None),
    )
    return jax.shard_map(local, mesh=mesh, in_specs=in_specs, out_specs=out_specs, check_vma=False)
```

profile of v0, /device:TPU:2, one launch (start us, length us, event | category | flops | bytes accessed | tf_op | source)
XLA Modules:
  0.0 991.1 jit_solution(17299420913924558690)
XLA Ops:
  8.3 3.5 collective-permute-start
  11.8 3.3 collective-permute-start.1
  15.1 5.2 collective-permute-done
  20.3 4.5 collective-permute-done.1
  26.6 1.7 fusion.50
  28.3 2.5 fusion.51
  30.8 2.4 fusion.52
  33.1 13.5 %concatenate.21 = bf16[2,32,32,864]{3,2,1,0:T(8,128)(2,1)} concatenate(bf16[2,32,32,32]{3,2,1,0:T(8,128)(2,1)} %get-tuple-element.77, bf16[2,32,32,32]{3,2,1,0:T(8,128)(2,1)} %get-tuple-element.76, bf16[2,32,32,32]{3,2,1,0:T(8,128)(2,1)} %get-tuple-element.75, bf16[2,32,32,32]{3,2,1,0:T(8,128)(2,1)} %get-tuple-element.74, bf16[2,32,32,32]{3,2,1,0:T(8,128)(2,1)} %get-tuple-element.73, ...), dimensions={3} | concatenate | bytes 7077888 | tf_op jit(solution)/shard_map/concatenate | solution.py:58
  46.6 4.8 fusion.57
  51.4 50.0 %reduce-scatter.3.cloned.1.call-done = f32[2048,32]{0,1:T(8,128)} async-done(((f32[2048,256]{0,1:T(8,128)}), f32[2048,32]{0,1:T(8,128)}) %reduce-scatter.3.cloned.1.call-update) | async-done | bytes 262160 | tf_op jit(solution)/shard_map/reduce_scatter | solution.py:75
  102.6 1.9 collective-permute-start.2
  104.7 4.8 collective-permute-start.3
  109.8 4.8 collective-permute-done.2
  114.6 3.9 collective-permute-done.3
  119.3 1.7 fusion.47
  121.0 2.4 fusion.48
  123.4 2.4 fusion.49
  125.7 13.4 %concatenate.23 = bf16[2,32,32,864]{3,2,1,0:T(8,128)(2,1)} concatenate(bf16[2,32,32,32]{3,2,1,0:T(8,128)(2,1)} %get-tuple-element.50, bf16[2,32,32,32]{3,2,1,0:T(8,128)(2,1)} %get-tuple-element.49, bf16[2,32,32,32]{3,2,1,0:T(8,128)(2,1)} %get-tuple-element.48, bf16[2,32,32,32]{3,2,1,0:T(8,128)(2,1)} %get-tuple-element.47, bf16[2,32,32,32]{3,2,1,0:T(8,128)(2,1)} %get-tuple-element.46, ...), dimensions={3} | concatenate | bytes 7077888 | tf_op jit(solution)/shard_map/concatenate | solution.py:58
  139.2 4.8 fusion.58
  144.1 10.4 %all-gather.3.cloned.1.call-start = ((), (), s32[]{:S(2)}) async-start(), calls=%async_computation.4 | async-start | bytes 4718592 | tf_op jit(solution)/shard_map/all_gather | solution.py:79
  154.9 34.0 %reduce-scatter.5.cloned.1.call-done = f32[2048,32]{0,1:T(8,128)} async-done(((f32[2048,256]{0,1:T(8,128)}), f32[2048,32]{0,1:T(8,128)}) %reduce-scatter.5.cloned.1.call-update) | async-done | bytes 262160 | tf_op jit(solution)/shard_map/reduce_scatter | solution.py:75
  191.8 51.5 %all-gather.3.cloned.1.call-done = bf16[2,32,32,256]{2,1,0,3:T(8,128)(2,1)} async-done(((bf16[2,32,32,32]{2,1,0,3:T(8,128)(2,1)}), bf16[2,32,32,256]{2,1,0,3:T(8,128)(2,1)}) %all-gather.3.cloned.1.call-update) | async-done | bytes 1048592 | tf_op jit(solution)/shard_map/all_gather | solution.py:79
  243.3 4.9 copy.43
  249.2 7.5 collective-permute-start.4
  256.7 1.9 collective-permute-start.5
  259.2 10.2 %collective-permute-done.4 = bf16[1,32,32,256]{3,2,1,0:T(8,128)(2,1)S(1)} collective-permute-done((bf16[1,32,32,256]{3,2,1,0:T(8,128)(2,1)}, bf16[1,32,32,256]{3,2,1,0:T(8,128)(2,1)S(1)}, u32[]{:S(2)}, u32[]{:S(2)}) %collective-permute-start.4) | collective-permute-done | bytes 524320 | tf_op jit(solution)/shard_map/ppermute | solution.py:20
  270.2 10.4 %collective-permute-done.5 = bf16[1,32,32,256]{3,2,1,0:T(8,128)(2,1)} collective-permute-done((bf16[1,32,32,256]{3,2,1,0:T(8,128)(2,1)S(1)}, bf16[1,32,32,256]{3,2,1,0:T(8,128)(2,1)}, u32[]{:S(2)}, u32[]{:S(2)}) %collective-permute-start.5) | collective-permute-done | bytes 524320 | tf_op jit(solution)/shard_map/ppermute | solution.py:23
  280.6 2.5 fusion.10
  284.6 1.7 slice_add_fusion.40
  287.9 1.7 reshape.285
  291.1 1.7 slice_add_fusion.32
  294.4 1.7 reshape.286
  302.0 6.1 copy.70
  308.1 6.1 copy.72
  315.2 37.4 %all-gather.5.cloned.1.call-done = bf16[2,32,32,256]{2,1,0,3:T(8,128)(2,1)} async-done(((bf16[2,32,32,32]{2,1,0,3:T(8,128)(2,1)}), bf16[2,32,32,256]{2,1,0,3:T(8,128)(2,1)}) %all-gather.5.cloned.1.call-update) | async-done | bytes 1048592 | tf_op jit(solution)/shard_map/all_gather | solution.py:79
  352.7 4.9 copy.49
  358.7 7.5 collective-permute-start.6
  366.1 1.9 collective-permute-start.7
  368.1 4.1 fusion.60
  372.2 2.0 fusion.59
  374.3 4.5 collective-permute-done.6
  378.8 11.2 %collective-permute-done.7 = bf16[1,32,32,256]{3,2,1,0:T(8,128)(2,1)} collective-permute-done((bf16[1,32,32,256]{3,2,1,0:T(8,128)(2,1)}, bf16[1,32,32,256]{3,2,1,0:T(8,128)(2,1)}, u32[]{:S(2)}, u32[]{:S(2)}) %collective-permute-start.7) | collective-permute-done | bytes 524320 | tf_op jit(solution)/shard_map/ppermute | solution.py:23
  390.0 2.3 select_maximum_fusion
  395.2 4.7 fusion.14
  400.0 7.4 fusion.31
  408.4 571.4 %all-reduce.7.cloned.1.call-done = (f32[3,3,3,32,256]{4,3,2,1,0:T(8,128)}, f32[3,3,3,32,256]{4,3,2,1,0:T(8,128)}) async-done(((f32[3,3,3,32,256]{4,3,2,1,0:T(8,128)}, f32[3,3,3,32,256]{4,3,2,1,0:T(8,128)}), (f32[3,3,3,32,256]{4,3,2,1,0:T(8,128)}, f32[3,3,3,32,256]{4,3,2,1,0:T(8,128)})) %all-reduce.7.cloned.1.call-update) | async-done | bytes 1769488 | tf_op jit(solution)/shard_map/psum | solution.py:111
  979.8 2.2 broadcast_multiply_fusion
  982.0 2.2 broadcast_multiply_fusion.1
  (67 shorter events, 29.1 us)
Async XLA Ops:
  7.2 94.3 %reduce-scatter.3.cloned.1.call-start = ((), (), s32[]{:S(2)}) async-start(), calls=%async_computation.2 | async-start | bytes 2359296 | tf_op jit(solution)/shard_map/reduce_scatter | solution.py:75
  8.3 12.0 %collective-permute-start = (bf16[1,32,32,32]{3,2,1,0:T(8,128)(2,1)S(1)}, bf16[1,32,32,32]{3,2,1,0:T(8,128)(2,1)S(1)}, u32[]{:S(2)}, u32[]{:S(2)}) collective-permute-start(bf16[1,32,32,32]{3,2,1,0:T(8,128)(2,1)S(1)} %get-tuple-element.78), channel_id=1, source_target_pairs={{0,1},{1,2},{2,3},{3,4},{4,5},{5,6},{6,7},{7,8},{8,9},{9,10},{10,1... | collective-permute-start | bytes 196616 | tf_op jit(solution)/shard_map/ppermute | solution.py:20
  11.8 13.0 %collective-permute-start.1 = (bf16[1,32,32,32]{3,2,1,0:T(8,128)(2,1)S(1)}, bf16[1,32,32,32]{3,2,1,0:T(8,128)(2,1)S(1)}, u32[]{:S(2)}, u32[]{:S(2)}) collective-permute-start(bf16[1,32,32,32]{3,2,1,0:T(8,128)(2,1)S(1)} %get-tuple-element.79), channel_id=1, source_target_pairs={{1,0},{2,1},{3,2},{4,3},{5,4},{6,5},{7,6},{8,7},{9,8},{10,9},{11,1... | collective-permute-start | bytes 196616 | tf_op jit(solution)/shard_map/ppermute | solution.py:23
  51.4 137.6 %reduce-scatter.5.cloned.1.call-start = ((), (), s32[]{:S(2)}) async-start(), calls=%async_computation.3 | async-start | bytes 2359296 | tf_op jit(solution)/shard_map/reduce_scatter | solution.py:75
  102.6 12.0 %collective-permute-start.2 = (bf16[1,32,32,32]{3,2,1,0:T(8,128)(2,1)S(1)}, bf16[1,32,32,32]{3,2,1,0:T(8,128)(2,1)S(1)}, u32[]{:S(2)}, u32[]{:S(2)}) collective-permute-start(bf16[1,32,32,32]{3,2,1,0:T(8,128)(2,1)S(1)} %bitcast.153), channel_id=1, source_target_pairs={{0,1},{1,2},{2,3},{3,4},{4,5},{5,6},{6,7},{7,8},{8,9},{9,10},{10,1... | collective-permute-start | bytes 196616 | tf_op jit(solution)/shard_map/ppermute | solution.py:20
  104.7 13.8 %collective-permute-start.3 = (bf16[1,32,32,32]{3,2,1,0:T(8,128)(2,1)S(1)}, bf16[1,32,32,32]{3,2,1,0:T(8,128)(2,1)S(1)}, u32[]{:S(2)}, u32[]{:S(2)}) collective-permute-start(bf16[1,32,32,32]{3,2,1,0:T(8,128)(2,1)S(1)} %bitcast.154), channel_id=1, source_target_pairs={{1,0},{2,1},{3,2},{4,3},{5,4},{6,5},{7,6},{8,7},{9,8},{10,9},{11,1... | collective-permute-start | bytes 196616 | tf_op jit(solution)/shard_map/ppermute | solution.py:23
  139.2 15.3 %copy-start.6 = (bf16[2,32,32,32]{3,2,1,0:T(8,128)(2,1)S(1)}, bf16[2,32,32,32]{3,2,1,0:T(8,128)(2,1)}, u32[]{:S(2)}) copy-start(bf16[2,32,32,32]{3,2,1,0:T(8,128)(2,1)} %param.7) | copy-start | bytes 393220
  144.1 99.3 %all-gather.3.cloned.1.call-start = ((), (), s32[]{:S(2)}) async-start(), calls=%async_computation.4 | async-start | bytes 4718592 | tf_op jit(solution)/shard_map/all_gather | solution.py:79
  191.8 67.3 %copy-start.3 = (bf16[3,3,3,32,256]{4,3,2,1,0:T(8,128)(2,1)S(1)}, bf16[3,3,3,32,256]{4,3,2,1,0:T(8,128)(2,1)}, u32[]{:S(2)}) copy-start(bf16[3,3,3,32,256]{4,3,2,1,0:T(8,128)(2,1)} %param.6) | copy-start | bytes 1327108
  191.8 160.9 %all-gather.5.cloned.1.call-start = ((), (), s32[]{:S(2)}) async-start(), calls=%async_computation.5 | async-start | bytes 4718592 | tf_op jit(solution)/shard_map/all_gather | solution.py:79
  248.3 21.1 %copy-start = (bf16[2,32,32,256]{3,2,1,0:T(8,128)(2,1)}, bf16[2,32,32,256]{3,2,1,0:T(8,128)(2,1)S(1)}, u32[]{:S(2)}) copy-start(bf16[2,32,32,256]{3,2,1,0:T(8,128)(2,1)S(1)} %copy.43) | copy-start | bytes 3145732
  249.2 20.1 %collective-permute-start.4 = (bf16[1,32,32,256]{3,2,1,0:T(8,128)(2,1)}, bf16[1,32,32,256]{3,2,1,0:T(8,128)(2,1)S(1)}, u32[]{:S(2)}, u32[]{:S(2)}) collective-permute-start(bf16[1,32,32,256]{3,2,1,0:T(8,128)(2,1)} %get-tuple-element.22), channel_id=1, source_target_pairs={{0,1},{1,2},{2,3},{3,4},{4,5},{5,6},{6,7},{7,8},{8,9},{9,10},{10,1... | collective-permute-start | bytes 1572872 | tf_op jit(solution)/shard_map/ppermute | solution.py:20
  256.7 23.9 %collective-permute-start.5 = (bf16[1,32,32,256]{3,2,1,0:T(8,128)(2,1)S(1)}, bf16[1,32,32,256]{3,2,1,0:T(8,128)(2,1)}, u32[]{:S(2)}, u32[]{:S(2)}) collective-permute-start(bf16[1,32,32,256]{3,2,1,0:T(8,128)(2,1)S(1)} %get-tuple-element.23), channel_id=1, source_target_pairs={{1,0},{2,1},{3,2},{4,3},{5,4},{6,5},{7,6},{8,7},{9,8},{10,9},{11,1... | collective-permute-start | bytes 1572872 | tf_op jit(solution)/shard_map/ppermute | solution.py:23
  269.4 0.8 copy-start.7
  299.3 1.3 copy-start.5
  299.3 2.6 copy-start.4
  301.9 677.9 %all-reduce.7.cloned.1.call-start = ((), (), s32[]{:S(2)}) async-start(), calls=%async_computation.6 | async-start | bytes 3538944 | tf_op jit(solution)/shard_map/psum | solution.py:111
  308.1 6.1 copy-start.8
  315.2 52.8 %copy-start.1 = (bf16[2,32,32,256]{3,2,1,0:T(8,128)(2,1)S(1)}, bf16[2,32,32,256]{3,2,1,0:T(8,128)(2,1)}, u32[]{:S(2)}) copy-start(bf16[2,32,32,256]{3,2,1,0:T(8,128)(2,1)} %copy-done) | copy-start | bytes 3145732
  358.7 20.1 %collective-permute-start.6 = (bf16[1,32,32,256]{3,2,1,0:T(8,128)(2,1)}, bf16[1,32,32,256]{3,2,1,0:T(8,128)(2,1)S(1)}, u32[]{:S(2)}, u32[]{:S(2)}) collective-permute-start(bf16[1,32,32,256]{3,2,1,0:T(8,128)(2,1)} %get-tuple-element.20), channel_id=1, source_target_pairs={{0,1},{1,2},{2,3},{3,4},{4,5},{5,6},{6,7},{7,8},{8,9},{9,10},{10,1... | collective-permute-start | bytes 1572872 | tf_op jit(solution)/shard_map/ppermute | solution.py:20
  366.1 23.9 %collective-permute-start.7 = (bf16[1,32,32,256]{3,2,1,0:T(8,128)(2,1)}, bf16[1,32,32,256]{3,2,1,0:T(8,128)(2,1)}, u32[]{:S(2)}, u32[]{:S(2)}) collective-permute-start(bf16[1,32,32,256]{3,2,1,0:T(8,128)(2,1)} %get-tuple-element.21), channel_id=1, source_target_pairs={{1,0},{2,1},{3,2},{4,3},{5,4},{6,5},{7,6},{8,7},{9,8},{10,9},{11,1... | collective-permute-start | bytes 1572872 | tf_op jit(solution)/shard_map/ppermute | solution.py:23
  368.1 4.2 copy-start.2
Sparse Core Ops, SparseCore 0:
  51.5 49.8 reduce-scatter.2
  144.2 44.7 reduce-scatter.4
  191.9 51.3 all-gather.2
  302.0 50.5 all-gather.4
  374.4 605.3 all-reduce.6
where the time goes:
time: 1000 us; the launch traced here: 991 us
  waiting for transfers between devices  799 us (80%)
  local copies, waits for them, and re-layouts  79.7 us (8%)
  starting transfers between devices  42.8 us (4%)
  matrix products  27.9 us (3%)
  other arithmetic  27.1 us (3%)
  between operations  14.5 us (1%)
    psum x1, waiting for transfers between devices, layer_sum(): return lax.psum(weight_grad, 'dp')  571 us
    all_gather x2, waiting for transfers between devices, backward(): wide = lax.all_gather(delta, 'chan', axis=3, tiled=True)  88.9 us
    reduce_scatter x2, waiting for transfers between devices, forward(): lax.psum_scatter(partial_value, 'chan', scatter_dimension=1, tiled=True)  84 us
    ppermute x4, waiting for transfers between devices, extended(): lax.ppermute(lax.slice_in_dim(block, 0, width, axis=dim), axis, backward)  30 us
    concatenate x2, local copies, waits for them, and re-layouts, columns(): stacked = jnp.concatenate(taps, axis=-1)  26.9 us
    ppermute x4, waiting for transfers between devices, extended(): lax.ppermute(lax.slice_in_dim(block, block.shape[dim] - width, None, axis...  24.7 us
    ppermute x4, starting transfers between devices, extended(): lax.ppermute(lax.slice_in_dim(block, block.shape[dim] - width, None, axis...  20.3 us
  transfers between devices with their start and end apart: 13, of which 13 were waited for; matrix products, arithmetic and copies ran while one was open for 4% of the time, Pallas kernels for 0%

commit v1 on v0

v1 whole, which is shorter than its diff:
```python
import functools
import math

import jax
import jax.numpy as jnp
from jax import lax
from jax.experimental import pallas as pl
from jax.experimental.pallas import tpu as pltpu
from jax.sharding import PartitionSpec as P

MESH = pl.DeviceIdType.MESH
SLOPE = 0.3
X, Y, Z = 4, 8, 8
N = 32
C = 256
HW = 1024
TAPS = 27
RP = 896
PART = RP // Z
SCALE = 1.0 / math.sqrt(4 * 32 * 32 * 32)
BF = jnp.bfloat16
F32 = jnp.float32


def shifted(x, rows, cols):
    pos = lax.broadcasted_iota(jnp.int32, x.shape, 1)
    off = rows * 32 + cols
    if off == 0:
        return x
    y = pltpu.roll(x, (-off) % HW, 1)
    ok = None
    if rows == 1:
        ok = pos < HW - 32
    if rows == -1:
        ok = pos >= 32
    if cols == 1:
        ok = (pos % 32) != 31
    if cols == -1:
        ok = (pos % 32) != 0
    return jnp.where(ok, y, jnp.zeros_like(y))


class Net:
    def __init__(self):
        chan = lax.axis_index("chan")
        dp = lax.axis_index("dp")
        self.c = chan
        self.core = chan % 2
        self.yl = dp % 2
        self.y = (chan // 2) * 2 + self.yl
        self.q = dp // 2
        self.x = self.q % X
        self.z = self.q // X
        self.dp = dp

    def dev(self, q, y, core):
        return {"chan": (y // 2) * 2 + core, "dp": q * 2 + y % 2}

    def in_ring(self, t, core):
        return self.dev(self.q, (self.y + t + Y) % Y, core)


class Copies:
    def __init__(self, send, recv, base):
        self.send, self.recv, self.next = send, recv, base
        self.started = []

    def slot(self):
        k = self.next
        self.next += 1
        return k

    def start(self, k, src, dst, device):
        cp = pltpu.make_async_remote_copy(
            src_ref=src,
            dst_ref=dst,
            send_sem=self.send.at[k],
            recv_sem=self.recv.at[k],
            device_id=device,
            device_id_type=MESH,
        )
        cp.start()
        self.started.append(cp)

    def wait(self, k, dst, device):
        pltpu.make_async_remote_copy(
            src_ref=dst,
            dst_ref=dst,
            send_sem=self.send.at[k],
            recv_sem=self.recv.at[k],
            device_id=device,
            device_id_type=MESH,
        ).wait_recv()

    def drain(self):
        for cp in self.started:
            cp.wait_send()
        self.started = []


def main_block(e, y, core):
    c = (y // 2) * 2 + core
    return e.at[pl.ds(1 + 2 * (y % 2), 2), pl.ds(pl.multiple_of(c * N, N), N), :]


def one_plane(e, plane, y, core):
    c = (y // 2) * 2 + core
    return e.at[pl.ds(plane, 1), pl.ds(pl.multiple_of(c * N, N), N), :]


def halo_block(e, y, core):
    return one_plane(e, 5 - 5 * (y % 2), y, core)


class Gather:
    def __init__(self, net, copies, e):
        self.net, self.cp, self.e = net, copies, e
        s = copies.slot
        self.k = {}
        for d in (1, -1):
            for t in (1, 2, 3, 4):
                self.k["main", d, t] = s()
                self.k["main", d, t, "sib"] = s()
            for t in (1, 2, 3):
                self.k["halo", d, t] = s()
                if t != 2:
                    self.k["halo", d, t, "sib"] = s()
        self.k["halo"] = s()
        self.k["own"] = s()

    def origin(self, d, t):
        return (self.net.y - d * t + Y) % Y

    def piece(self, kind, d, t, core):
        y = self.origin(d, t)
        if kind == "halo":
            return halo_block(self.e, y, core)
        if t == 4:
            plane = 1 + 2 * (y % 2) + (0 if d == 1 else 1)
            return one_plane(self.e, plane, y, core)
        return main_block(self.e, y, core)

    def send_on(self, kind, d, t, core):
        y = self.origin(d, t - 1)
        if kind == "halo":
            ref = halo_block(self.e, y, core)
        elif t == 4:
            plane = 1 + 2 * (y % 2) + (0 if d == 1 else 1)
            ref = one_plane(self.e, plane, y, core)
        else:
            ref = main_block(self.e, y, core)
        self.cp.start(self.k[kind, d, t], ref, ref, self.net.in_ring(d, core))

    def start(self):
        n, e = self.net, self.e
        step = 2 * n.yl - 1
        q = (n.q + step + X * Z) % (X * Z)
        self.far = n.dev(q, n.y, n.core)
        self.cp.start(
            self.k["halo"],
            one_plane(e, 1 + 3 * n.yl, n.y, n.core),
            halo_block(e, n.y, n.core),
            n.dev(q, n.y, n.core),
        )
        self.send_on("main", 1, 1, n.core)
        self.send_on("main", -1, 1, n.core)
        own = main_block(e, n.y, n.core)
        self.cp.start(self.k["own"], own, own, n.in_ring(0, 1 - n.core))

    def got(self, kind, d, t):
        n = self.net
        ref = self.piece(kind, d, t, n.core)
        self.cp.wait(self.k[kind, d, t], ref, n.in_ring(-d, n.core))
        if t < (3 if kind == "halo" else 4):
            self.send_on(kind, d, t + 1, n.core)
        if kind == "main" or t != 2:
            self.cp.start(self.k[kind, d, t, "sib"], ref, ref, n.in_ring(0, 1 - n.core))

    def run(self):
        n = self.net
        both = (1, -1)
        for d in both:
            self.got("main", d, 1)
        ref = halo_block(self.e, n.y, n.core)
        self.cp.wait(self.k["halo"], ref, self.far)
        for d in both:
            self.send_on("halo", d, 1, n.core)
        for t in (2, 3, 4):
            for d in both:
                self.got("main", d, t)
            for d in both:
                self.got("halo", d, t - 1)
        sib = n.in_ring(0, 1 - n.core)
        other = 1 - n.core
        self.cp.wait(self.k["own"], main_block(self.e, n.y, other), sib)
        for d in both:
            for t in (1, 2, 3, 4):
                self.cp.wait(self.k["main", d, t, "sib"], self.piece("main", d, t, other), sib)
            for t in (1, 3):
                self.cp.wait(self.k["halo", d, t, "sib"], self.piece("halo", d, t, other), sib)
        self.cp.drain()


class Turn:
    def __init__(self, net, copies, src, dst):
        self.net, self.cp, self.src, self.dst = net, copies, src, dst
        self.k = {(t, rc): copies.slot() for t in (1, 2, 3) for rc in (0, 1)}
        self.k[0] = copies.slot()

    def rows(self, c):
        return self.dst.at[pl.ds(pl.multiple_of(c * N, N), N), :]

    def start(self):
        n = self.net
        way = 2 * n.yl - 1
        for t in (1, 2, 3):
            y = (n.y + way * t + Y) % Y
            for rc in (0, 1):
                core = (n.core + rc) % 2
                c = (y // 2) * 2 + core
                self.cp.start(self.k[t, rc], self.src.at[c], self.rows(n.c), n.dev(n.q, y, core))
        other = (n.y // 2) * 2 + 1 - n.core
        self.cp.start(self.k[0], self.src.at[other], self.rows(n.c), n.in_ring(0, 1 - n.core))
        self.dst[pl.ds(pl.multiple_of(n.c * N, N), N), :] = self.src[n.c]

    def finish(self):
        n = self.net
        way = 2 * n.yl - 1
        for t in (1, 2, 3):
            y = (n.y + (way * t if t != 2 else -way * t) + Y) % Y
            for rc in (0, 1):
                core = (n.core + rc) % 2
                c = (y // 2) * 2 + core
                self.cp.wait(self.k[t, rc], self.rows(c), n.dev(n.q, y, core))
        other = (n.y // 2) * 2 + 1 - n.core
        self.cp.wait(self.k[0], self.rows(other), n.in_ring(0, 1 - n.core))
        self.cp.drain()


class Reduce:
    def __init__(self, net, copies, part, r1, b2, r2, s2, x4, fin, out):
        self.net, self.cp = net, copies
        self.part, self.r1, self.b2, self.r2, self.s2 = part, r1, b2, r2, s2
        self.x4, self.fin, self.out = x4, fin, out
        self.ka = [copies.slot() for _ in range(Z - 1)]
        self.kb = copies.slot()
        self.kc = [copies.slot() for _ in range(X - 1)]
        self.kd = copies.slot()
        self.ke = [copies.slot() for _ in range(Z - 1)]

    def zdev(self, t):
        n = self.net
        return n.dev(((n.z + t + Z) % Z) * X + n.x, n.y, n.core)

    def xdev(self, t):
        n = self.net
        return n.dev(n.z * X + (n.x + t + X) % X, n.y, n.core)

    def pair(self):
        n = self.net
        return n.dev(n.q, n.y + 1 - 2 * n.yl, n.core)

    def start(self):
        n = self.net
        for t in range(1, Z):
            self.cp.start(self.ka[t - 1], self.part.at[(n.z + t) % Z], self.r1.at[t - 1], self.zdev(t))

    def sum_z(self):
        n = self.net
        total = self.part[n.z].astype(F32)
        for t in range(1, Z):
            self.cp.wait(self.ka[t - 1], self.r1.at[t - 1], self.zdev(-t))
            total = total + self.r1[t - 1].astype(F32)
        for h in (0, 1):
            half = total[:, h * 128 : (h + 1) * 128]
            self.s2[h] = half
            self.b2[h] = half.astype(BF)
        self.cp.start(self.kb, self.b2.at[1 - n.yl], self.r2, self.pair())

    def sum_y(self):
        n = self.net
        self.cp.wait(self.kb, self.r2, self.pair())
        self.x4[n.x] = (self.s2[n.yl] + self.r2[...].astype(F32)).astype(BF)
        for t in range(1, X):
            self.cp.start(self.kc[t - 1], self.x4.at[n.x], self.x4.at[n.x], self.xdev(t))

    def sum_x(self):
        n = self.net
        for t in range(1, X):
            self.cp.wait(self.kc[t - 1], self.x4.at[(n.x - t + X) % X], self.xdev(-t))
        total = self.x4[0].astype(F32)
        for x in range(1, X):
            total = total + self.x4[x].astype(F32)
        self.fin[n.z, n.yl] = total.astype(BF)
        ref = self.fin.at[n.z, n.yl]
        self.cp.start(self.kd, ref, ref, self.pair())

    def spread(self):
        n = self.net
        self.cp.wait(self.kd, self.fin.at[n.z, 1 - n.yl], self.pair())
        for t in range(1, Z):
            self.cp.start(self.ke[t - 1], self.fin.at[n.z], self.fin.at[n.z], self.zdev(t))

    def finish(self):
        n = self.net
        for t in range(1, Z):
            self.cp.wait(self.ke[t - 1], self.fin.at[(n.z - t + Z) % Z], self.zdev(-t))
        for z in range(Z):
            rows = min(PART, TAPS * N - z * PART)
            for h in (0, 1):
                self.out[z * PART : z * PART + rows, h * 128 : (h + 1) * 128] = (
                    self.fin[z, h, :rows].astype(F32) * SCALE
                )
        self.cp.drain()


def conv(w, e, base, s, sign, use):
    for j in (0, 1):

        @pl.loop(0, HW // 256)
        def _(t):
            lanes = pl.ds(pl.multiple_of(t * 256, 256), 256)
            planes = e[pl.ds(base + j, 3), :, lanes].reshape(3 * C, 256)
            s[:, lanes] = jnp.dot(w[j], planes, preferred_element_type=F32)

        total = None
        for c in range(3):
            line = None
            for b in range(3):
                at = (b * 3 + c) * N
                term = shifted(s[at : at + N, :], sign * (b - 1), 0)
                line = term if line is None else line + term
            line = shifted(line, 0, sign * (c - 1))
            total = line if total is None else total + line
        use(j, total)


def grad_columns(e, c, base, joined, a):
    for slot in range(4):
        plane = e[base + slot, pl.ds(pl.multiple_of(c * N, N), N), :].astype(F32)
        for col in range(3):
            moved = shifted(plane, 0, col - 1)
            for row in range(3):
                value = shifted(moved, row - 1, 0)
                for j in (0, 1):
                    depth = slot - j
                    if 0 <= depth < 3:
                        v = value * joined if (j, depth) in ((0, 2), (1, 0)) else value
                        at = (depth * 9 + row * 3 + col) * N
                        a[j, at : at + N, :] = v.astype(BF)


def grad_part(a, e, base, part):
    nt = (((1,), (1,)), ((), ()))
    one = e[base + 1]
    two = e[base + 2]
    for z in range(Z):
        rows = min(PART, TAPS * N - z * PART)
        at = slice(z * PART, z * PART + rows)
        g = lax.dot_general(a[0, at], one, nt, preferred_element_type=F32)
        g = g + lax.dot_general(a[1, at], two, nt, preferred_element_type=F32)
        part[z, :rows] = g.astype(BF)
        if rows < PART:
            part[z, rows:] = jnp.zeros((PART - rows, C), BF)


def filter_rows(block, joined, at, w):
    lanes = slice(at * C, (at + 1) * C)
    masked = (block.astype(F32) * joined).astype(BF)
    w[0, :, lanes] = masked if at == 2 else block
    w[1, :, lanes] = masked if at == 0 else block


def forward_filter(turned, joined, w):
    rows = turned[...].astype(F32).T
    for a in range(3):
        filter_rows(rows[a * 288 : (a + 1) * 288].astype(BF), joined, a, w)


def backward_filter(own, joined, w):
    for a in range(3):
        filter_rows(own[(2 - a) * 288 : (3 - a) * 288, :], joined, a, w)


def whole(
    vol, cot, own1, own2, out1, out2,
    output, input_grad, g1, g2,
    e1, e2, e3, e4, t1, t2, wf1, wf2, wb1, wb2, s, pre, a, part1, part2,
    r1, b2, r2, s2, x4, fin, send, recv,
):
    net = Net()
    barrier = pltpu.get_barrier_semaphore()
    greeted = [net.in_ring(t, core) for t in range(1, Y) for core in (0, 1)]
    greeted.append(net.in_ring(0, 1 - net.core))
    total = X * Z
    for t in range(1, Z):
        greeted.append(net.dev(((net.z + t) % Z) * X + net.x, net.y, net.core))
    for t in range(1, X):
        greeted.append(net.dev(net.z * X + (net.x + t) % X, net.y, net.core))
    for t in (1, -1):
        greeted.append(net.dev((net.q + t + total) % total, net.y, net.core))
    for device in greeted:
        pl.semaphore_signal(barrier, inc=1, device_id=device, device_id_type=MESH)
    pl.semaphore_wait(barrier, len(greeted))

    base = 2 * net.yl
    joined = jnp.where(net.dp % 16 == 0, 0.0, 1.0).astype(F32)

    def own(e):
        return pl.ds(pl.multiple_of(net.c * N, N), N)

    even, odd = Copies(send, recv, 0), Copies(send, recv, 29)
    turn1 = Turn(net, Copies(send, recv, 58), out1, t1)
    turn2 = Turn(net, Copies(send, recv, 65), out2, t2)
    gathers = []
    for i, e in enumerate((e1, e2, e3, e4)):
        gathers.append(Gather(net, Copies(send, recv, (i % 2) * 29), e))
    red2 = Reduce(net, Copies(send, recv, 72), part2, r1.at[1], b2.at[1], r2.at[1], s2.at[1], x4.at[1], fin.at[1], g2)
    red1 = Reduce(net, Copies(send, recv, 91), part1, r1.at[0], b2.at[0], r2.at[0], s2.at[0], x4.at[0], fin.at[0], g1)

    for j in (0, 1):
        e1[base + 1 + j, own(e1), :] = vol[j]
    turn1.start()
    gathers[0].start()
    backward_filter(own1, joined, wb1)
    backward_filter(own2, joined, wb2)
    gathers[0].run()
    turn1.finish()
    turn2.start()
    forward_filter(t1, joined, wf1)

    def after_one(j, v):
        pre[j] = jnp.where(v > 0, jnp.float32(1.0), jnp.float32(SLOPE))
        e2[base + 1 + j, own(e2), :] = jnp.where(v > 0, v, SLOPE * v).astype(BF)

    conv(wf1, e1, base, s, 1, after_one)

    gathers[1].start()
    gathers[1].run()
    turn2.finish()
    forward_filter(t2, joined, wf2)

    def after_two(j, v):
        output[j] = jnp.where(v > 0, v, SLOPE * v).astype(BF)
        slope = jnp.where(v > 0, jnp.float32(1.0), jnp.float32(SLOPE))
        e3[base + 1 + j, own(e3), :] = (cot[j].astype(F32) * slope).astype(BF)

    conv(wf2, e2, base, s, 1, after_two)

    gathers[2].start()
    grad_columns(e2, net.c, base, joined, a)
    gathers[2].run()

    def after_back(j, v):
        e4[base + 1 + j, own(e4), :] = (v * pre[j]).astype(BF)

    conv(wb2, e3, base, s, -1, after_back)

    gathers[3].start()
    grad_part(a, e3, base, part2)
    red2.start()
    grad_columns(e1, net.c, base, joined, a)
    gathers[3].run()
    red2.sum_z()
    grad_part(a, e4, base, part1)
    red1.start()
    red2.sum_y()

    def last(j, v):
        input_grad[j] = v.astype(BF)

    conv(wb1, e4, base, s, -1, last)
    red2.sum_x()
    red1.sum_z()
    red2.spread()
    red1.sum_y()
    red1.sum_x()
    red2.finish()
    red1.spread()
    red1.finish()


def local(volume, filter_one, filter_two, cotangent):
    def planes(v):
        return v.transpose(0, 3, 1, 2).reshape(2, N, HW)

    def back(v):
        return v.reshape(2, N, 32, 32).transpose(0, 2, 3, 1)

    def by_owner(w):
        w = w.reshape(TAPS, N, 8, N).transpose(2, 1, 0, 3).reshape(8, N, TAPS * N)
        return jnp.pad(w, ((0, 0), (0, 0), (0, RP - TAPS * N)))

    vm = pl.BlockSpec(memory_space=pltpu.VMEM)
    shape = jax.ShapeDtypeStruct
    output, input_grad, g1, g2 = pl.pallas_call(
        whole,
        out_shape=(
            shape((2, N, HW), BF),
            shape((2, N, HW), BF),
            shape((TAPS * N, C), F32),
            shape((TAPS * N, C), F32),
        ),
        in_specs=[vm] * 6,
        out_specs=[vm] * 4,
        scratch_shapes=[
            pltpu.VMEM((6, C, HW), BF),
            pltpu.VMEM((6, C, HW), BF),
            pltpu.VMEM((6, C, HW), BF),
            pltpu.VMEM((6, C, HW), BF),
            pltpu.VMEM((C, RP), BF),
            pltpu.VMEM((C, RP), BF),
            pltpu.VMEM((2, 288, 3 * C), BF),
            pltpu.VMEM((2, 288, 3 * C), BF),
            pltpu.VMEM((2, 288, 3 * C), BF),
            pltpu.VMEM((2, 288, 3 * C), BF),
            pltpu.VMEM((288, HW), F32),
            pltpu.VMEM((2, N, HW), F32),
            pltpu.VMEM((2, TAPS * N, HW), BF),
            pltpu.VMEM((Z, PART, C), BF),
            pltpu.VMEM((Z, PART, C), BF),
            pltpu.VMEM((2, Z - 1, PART, C), BF),
            pltpu.VMEM((2, 2, PART, 128), BF),
            pltpu.VMEM((2, PART, 128), BF),
            pltpu.VMEM((2, 2, PART, 128), F32),
            pltpu.VMEM((2, X, PART, 128), BF),
            pltpu.VMEM((2, Z, 2, PART, 128), BF),
            pltpu.SemaphoreType.DMA((110,)),
            pltpu.SemaphoreType.DMA((110,)),
        ],
        compiler_params=pltpu.CompilerParams(
            collective_id=0, has_side_effects=True, vmem_limit_bytes=50 * 1024 * 1024
        ),
    )(
        planes(volume),
        planes(cotangent),
        filter_one.reshape(TAPS * N, C),
        filter_two.reshape(TAPS * N, C),
        by_owner(filter_one),
        by_owner(filter_two),
    )
    filters = (3, 3, 3, N, C)
    return back(output), back(input_grad), g1.reshape(filters), g2.reshape(filters)


def solution(mesh):
    rows = P("dp", None, None, "chan")
    filters = P(None, None, None, "chan", None)
    return jax.shard_map(
        local,
        mesh=mesh,
        in_specs=(rows, filters, filters, rows),
        out_specs=(rows, rows, filters, filters),
        check_vma=False,
    )
```

time: 1000 us -> 192 us (0.19)
  the two profiles are of different devices: /device:TPU:2 before, /device:TPU:1 now
where the time goes in v1:
time: 192 us
  Pallas kernels  168 us (88%)
  local copies, waits for them, and re-layouts  22.5 us (12%)
    pallas_call x1, Pallas kernels, local(): pl.pallas_call(whole, out_shape=(shape((2, N, HW), BF), shape((2, N, HW),...  168 us
    reshape x6, local copies, waits for them, and re-layouts, by_owner(): w = w.reshape(TAPS, N, 8, N).transpose(2, 1, 0, 3).reshape(8, N, TAPS * N)  13.9 us
    unnamed x8, local copies, waits for them, and re-layouts  4 us

profile of v1, /device:TPU:1, one launch (start us, length us, event | category | flops | bytes accessed | tf_op | source)
XLA Modules:
  0.0 191.6 jit_solution(11355926834637610691)
XLA Ops:
  0.6 3.1 %reshape.48 = bf16[27,32,8,32]{3,2,1,0:T(8,128)(2,1)} reshape(bf16[3,3,3,32,256]{4,3,2,1,0:T(8,128)(2,1)} %param.5) | data formatting | bytes 884736 | tf_op jit(solution)/shard_map/reshape | solution.py:491
  3.7 2.7 %copy.27 = bf16[27,32,8,32]{3,0,1,2:T(8,128)(2,1)S(1)} copy(bf16[27,32,8,32]{3,2,1,0:T(8,128)(2,1)} %reshape.48) | data formatting | bytes 884736 | tf_op jit(solution)/shard_map/reshape | solution.py:491
  6.4 0.0 copy-start.1
  6.4 1.7 reshape.49
  8.2 0.0 copy-done.1
  8.2 0.8 reshape.50
  8.9 2.5 %copy.26 = bf16[27,32,8,32]{3,0,1,2:T(8,128)(2,1)} copy(bf16[27,32,8,32]{3,2,1,0:T(8,128)(2,1)S(1)} %reshape.50) | data formatting | bytes 884736 | tf_op jit(solution)/shard_map/reshape | solution.py:491
  11.5 0.0 copy-start
  11.5 3.2 %reshape.51 = bf16[8,32,864]{2,1,0:T(8,128)(2,1)S(1)} reshape(bf16[8,32,27,32]{3,2,1,0:T(8,128)(2,1)} %bitcast.31) | data formatting | bytes 884736 | tf_op jit(solution)/shard_map/reshape | solution.py:491
  14.7 1.2 copy.20.vol
  15.9 1.2 copy.21.cot
  17.2 0.0 copy-done
  17.2 168.4 %shard_map.75 = (bf16[2,32,1024]{2,1,0:T(8,128)(2,1)S(1)}, bf16[2,32,1024]{2,1,0:T(8,128)(2,1)S(1)}, f32[864,256]{1,0:T(8,128)S(1)}, f32[864,256]{1,0:T(8,128)S(1)}) custom-call(bf16[2,32,1024]{2,1,0:T(8,128)(2,1)S(1)} %copy.20.vol, bf16[2,32,1024]{2,1,0:T(8,128)(2,1)S(1)} %copy.21.cot, bf16[864,256]{1,0:T(8,128)(2,1)S(1)} %bitcast.26, ...), custom_call_target="tpu_custom_call" | custom-call | tf_op jit(solution)/shard_map/pallas_call | solution.py:496
  185.6 0.0 copy-start.2
  185.6 0.9 copy-done.2
  186.5 1.0 copy.23
  187.5 1.0 copy.22
  188.5 2.2 %copy.30 = f32[3,3,3,32,256]{4,3,2,1,0:T(8,128)} copy(f32[3,3,3,32,256]{4,3,2,1,0:T(8,128)} %bitcast.29) | data formatting | bytes 1769472
  190.7 0.9 copy.31
  (2 shorter events, 0.1 us)
Async XLA Ops:
  6.4 1.8 copy-start.1
  11.5 5.7 %copy-start = (bf16[3,3,3,32,256]{4,3,2,1,0:T(8,128)(2,1)S(1)}, bf16[3,3,3,32,256]{4,3,2,1,0:T(8,128)(2,1)}, u32[]{:S(2)}) copy-start(bf16[3,3,3,32,256]{4,3,2,1,0:T(8,128)(2,1)} %param.5) | copy-start | bytes 1327108
  185.6 0.9 copy-start.2

commit v2 on v1

v2 whole, which is shorter than its diff:
```python
import functools
import math

import jax
import jax.numpy as jnp
from jax import lax
from jax.experimental import pallas as pl
from jax.experimental.pallas import tpu as pltpu
from jax.sharding import PartitionSpec as P

MESH = pl.DeviceIdType.MESH
SLOPE = 0.3
X, Y, Z = 4, 8, 8
N = 32
C = 256
HW = 1024
TAPS = 27
SHARE = 7
SCALE = 1.0 / math.sqrt(4 * 32 * 32 * 32)
BF = jnp.bfloat16
F32 = jnp.float32


def shifted(x, rows, cols):
    pos = lax.broadcasted_iota(jnp.int32, x.shape, 1)
    off = rows * 32 + cols
    if off == 0:
        return x
    y = pltpu.roll(x, (-off) % HW, 1)
    ok = None
    if rows == 1:
        ok = pos < HW - 32
    if rows == -1:
        ok = pos >= 32
    if cols == 1:
        ok = (pos % 32) != 31
    if cols == -1:
        ok = (pos % 32) != 0
    return jnp.where(ok, y, jnp.zeros_like(y))


class Net:
    def __init__(self):
        chan = lax.axis_index("chan")
        dp = lax.axis_index("dp")
        self.c = chan
        self.core = chan % 2
        self.yl = dp % 2
        self.y = (chan // 2) * 2 + self.yl
        self.q = dp // 2
        self.x = self.q % X
        self.z = self.q // X
        self.dp = dp

    def dev(self, q, y, core):
        return {"chan": (y // 2) * 2 + core, "dp": q * 2 + y % 2}

    def xdev(self, t):
        return self.dev(self.z * X + (self.x + t + X) % X, self.y, self.core)

    def zdev(self, t):
        return self.dev(((self.z + t + Z) % Z) * X + self.x, self.y, self.core)

    def in_ring(self, t, core):
        return self.dev(self.q, (self.y + t + Y) % Y, core)


class Copies:
    def __init__(self, send, recv, base):
        self.send, self.recv, self.next = send, recv, base
        self.started = []

    def slot(self):
        k = self.next
        self.next += 1
        return k

    def start(self, k, src, dst, device):
        cp = pltpu.make_async_remote_copy(
            src_ref=src,
            dst_ref=dst,
            send_sem=self.send.at[k],
            recv_sem=self.recv.at[k],
            device_id=device,
            device_id_type=MESH,
        )
        cp.start()
        self.started.append(cp)

    def wait(self, k, dst, device):
        pltpu.make_async_remote_copy(
            src_ref=dst,
            dst_ref=dst,
            send_sem=self.send.at[k],
            recv_sem=self.recv.at[k],
            device_id=device,
            device_id_type=MESH,
        ).wait_recv()

    def drain(self):
        for cp in self.started:
            cp.wait_send()
        self.started = []


def block(e, slot, y, core):
    c = (y // 2) * 2 + core
    return e.at[slot, pl.ds(pl.multiple_of(c * N, N), N), :]


class Gather:
    BOTH = (1, -1)

    def __init__(self, net, copies, e):
        self.net, self.cp, self.e = net, copies, e
        self.k = {}
        s = copies.slot
        for kind in ("outer", "inner"):
            self.k[kind] = s()
            for d in self.BOTH:
                for t in (1, 2, 3, 4):
                    if t < 4 or (kind == "outer") == (d == 1):
                        self.k[kind, d, t] = s()
                        if kind == "inner" or t % 2 == 0:
                            self.k[kind, d, t, "sib"] = s()
                    if kind == "outer" and t % 2 == 1:
                        self.k["far", d, t] = s()
                        self.k["far", d, t, "sib"] = s()

    def at(self, kind, d, t, core):
        y = (self.net.y - d * t + Y) % Y
        if kind == "far":
            return block(self.e, 5 * self.net.yl, y, core)
        return block(self.e, 1 + 3 * (y % 2) if kind == "outer" else 2 + y % 2, y, core)

    def sibling(self):
        return self.net.in_ring(0, 1 - self.net.core)

    def pass_on(self, kind, d, t):
        ref = self.at(kind, d, t - 1, self.net.core)
        self.cp.start(self.k[kind, d, t], ref, ref, self.net.in_ring(d, self.net.core))

    def start(self, kinds=("inner", "outer")):
        for kind in kinds:
            for d in self.BOTH:
                self.pass_on(kind, d, 1)
            ref = self.at(kind, 1, 0, self.net.core)
            self.cp.start(self.k[kind], ref, ref, self.sibling())

    def share(self, kind, d, t):
        ref = self.at(kind, d, t, self.net.core)
        self.cp.start(self.k[kind, d, t, "sib"], ref, ref, self.sibling())

    def got(self, kind, d, t):
        n = self.net
        ref = self.at(kind, d, t, n.core)
        self.cp.wait(self.k[kind, d, t], ref, n.in_ring(-d, n.core))
        if (kind, d, t + 1) in self.k:
            self.pass_on(kind, d, t + 1)
        if kind == "outer" and t % 2 == 1:
            q = (n.q + 1 - 2 * n.yl + X * Z) % (X * Z)
            self.cp.start(self.k["far", d, t], ref, self.at("far", d, t, n.core), n.dev(q, n.y, n.core))
        if (kind, d, t, "sib") in self.k:
            self.share(kind, d, t)

    def far(self, t):
        n = self.net
        q = (n.q - 1 + 2 * n.yl + X * Z) % (X * Z)
        for d in self.BOTH:
            self.cp.wait(self.k["far", d, t], self.at("far", d, t, n.core), n.dev(q, n.y, n.core))
            self.share("far", d, t)

    def step(self, t):
        for kind in ("inner", "outer"):
            for d in self.BOTH:
                if (kind, d, t) in self.k:
                    self.got(kind, d, t)
        if t >= 3:
            self.far(2 * t - 5)

    def most(self):
        other = 1 - self.net.core
        for kind in ("inner", "outer"):
            self.cp.wait(self.k[kind], self.at(kind, 1, 0, other), self.sibling())
        self.from_sibling(("inner", "outer"))

    def from_sibling(self, kinds):
        for key in self.k:
            if len(key) == 4 and key[0] in kinds:
                self.cp.wait(self.k[key], self.at(*key[:3], 1 - self.net.core), self.sibling())

    def rest(self):
        self.from_sibling(("far",))


class Turn:
    def __init__(self, net, copies, src, dst, me, shares, peer):
        self.net, self.cp, self.src, self.dst = net, copies, src, dst
        self.me, self.shares, self.peer = me, shares, peer
        self.k = {(t, rc): copies.slot() for t in (1, 2, 3) for rc in (0, 1)}
        self.k[0] = copies.slot()
        self.kp = [copies.slot() for _ in range(shares - 1)]

    def rows(self, c):
        return self.dst.at[self.me, pl.ds(pl.multiple_of(c * N, N), N), :]

    def cut(self, own):
        lanes = self.src.shape[2]
        count = lanes // N
        pos = lax.broadcasted_iota(jnp.int32, (N, lanes), 1) // N
        made = [None] * 8
        for k in range(count):
            tap = jnp.minimum(self.me * count + k, TAPS - 1)
            v = own[pl.ds(pl.multiple_of(tap * N, N), N), :].astype(F32)
            for c in range(8):
                r = pltpu.roll(v, ((k - c) % 8) * N, 1) if k != c else v
                r = r[:, :lanes]
                made[c] = r if k == 0 else jnp.where(pos == k, r, made[c])
        for c in range(8):
            self.src[c] = made[c].astype(BF)

    def start(self):
        n = self.net
        way = 2 * n.yl - 1
        for t in (1, 2, 3):
            y = (n.y + way * t + Y) % Y
            for rc in (0, 1):
                core = (n.core + rc) % 2
                c = (y // 2) * 2 + core
                self.cp.start(self.k[t, rc], self.src.at[c], self.rows(n.c), n.dev(n.q, y, core))
        other = (n.y // 2) * 2 + 1 - n.core
        self.cp.start(self.k[0], self.src.at[other], self.rows(n.c), n.in_ring(0, 1 - n.core))
        self.dst[self.me, pl.ds(pl.multiple_of(n.c * N, N), N), :] = self.src[n.c]

    def spread(self):
        n = self.net
        way = 2 * n.yl - 1
        for t in (1, 2, 3):
            y = (n.y + (way * t if t != 2 else -way * t) + Y) % Y
            for rc in (0, 1):
                core = (n.core + rc) % 2
                c = (y // 2) * 2 + core
                self.cp.wait(self.k[t, rc], self.rows(c), n.dev(n.q, y, core))
        other = (n.y // 2) * 2 + 1 - n.core
        self.cp.wait(self.k[0], self.rows(other), n.in_ring(0, 1 - n.core))
        ref = self.dst.at[self.me]
        for t in range(1, self.shares):
            self.cp.start(self.kp[t - 1], ref, ref, self.peer(t))

    def finish(self):
        for t in range(1, self.shares):
            ref = self.dst.at[(self.me - t + self.shares) % self.shares]
            self.cp.wait(self.kp[t - 1], ref, self.peer(-t))
        self.cp.drain()

    def filters(self, joined, w):
        count = self.src.shape[2] // N
        for share in range(-(-TAPS // count)):
            rows = self.dst[share].astype(F32).T
            for k in range(min(count, TAPS - share * count)):
                tap = share * count + k
                filter_rows(rows[k * N : (k + 1) * N], joined, tap // 9, (tap % 9) * N, w)


class Reduce:
    def __init__(self, net, copies, part, r1, p2, r2, q, rq, fin, out):
        self.net, self.cp = net, copies
        self.part, self.r1, self.p2, self.r2 = part, r1, p2, r2
        self.q, self.rq, self.fin, self.out = q, rq, fin, out
        self.others = [(t, h) for t in range(Z) for h in (0, 1) if (t, h) != (0, 0)]
        self.ka = [copies.slot() for _ in range(X - 1)]
        self.kb = [copies.slot() for _ in self.others]
        self.kc = [copies.slot() for _ in range(8)]
        self.kd = [copies.slot() for _ in range(Z - 1)]
        self.ke = [copies.slot() for _ in range(X - 1)]

    def peer(self, t, h):
        n = self.net
        y = n.y + (h - 2 * h * n.yl)
        return n.dev(((n.z + t + Z) % Z) * X + n.x, y, n.core)

    def start(self):
        n = self.net
        for t in range(1, X):
            src = self.part.at[(n.x + t) % X]
            self.cp.start(self.ka[t - 1], src, self.r1.at[t - 1], n.xdev(t))

    def sum_x(self):
        n = self.net
        for t in range(1, X):
            self.cp.wait(self.ka[t - 1], self.r1.at[t - 1], n.xdev(-t))
        total = self.part[n.x].astype(F32)
        for t in range(1, X):
            total = total + self.r1[t - 1].astype(F32)
        for z in range(SHARE):
            for h in (0, 1):
                self.p2[z, h] = total[z * N : (z + 1) * N, h * 128 : (h + 1) * 128].astype(BF)
        for i, (t, h) in enumerate(self.others):
            src = self.p2.at[(n.z + t) % Z, (n.yl + h) % 2]
            self.cp.start(self.kb[i], src, self.r2.at[i], self.peer(t, h))

    def turns(self):
        n = self.net
        for h in (0, 1):
            for m in range(4):
                c = 4 * n.yl + m
                yield h, m, c, {"chan": c, "dp": n.q * 2 + (n.yl + h) % 2}

    def turn_copy(self, h, m, device):
        return pltpu.make_async_remote_copy(
            src_ref=self.q.at[pl.ds(m * N, N), :],
            dst_ref=self.rq.at[self.net.c],
            send_sem=self.cp.send.at[self.kc[4 * h + m]],
            recv_sem=self.cp.recv.at[self.kc[0] + self.net.c],
            device_id=device,
            device_id_type=MESH,
        )

    def sum_z(self):
        n = self.net
        for i, (t, h) in enumerate(self.others):
            self.cp.wait(self.kb[i], self.r2.at[i], self.peer(-t, h))
        total = self.p2[n.z, n.yl].astype(F32)
        for i in range(len(self.others)):
            total = total + self.r2[i].astype(F32)
        square = jnp.concatenate([total, jnp.zeros((128 - N, 128), F32)], axis=0)
        self.q[...] = square.T.astype(BF)
        for h, m, c, device in self.turns():
            if h:
                self.turn_copy(h, m, device).start()
                continue

            @pl.when(c != n.c)
            def _():
                self.turn_copy(h, m, device).start()

            @pl.when(c == n.c)
            def _():
                self.rq[n.c] = self.q[m * N : (m + 1) * N, :]

    def collect(self):
        n = self.net
        half = n.c // 4
        for c in range(8):

            @pl.when(jnp.logical_or(c != n.c, half != n.yl))
            def _():
                self.cp.wait(self.kc[c], self.rq.at[c], {"chan": c, "dp": n.q * 2 + half})

        for h, m, c, device in self.turns():
            if h:
                self.turn_copy(h, m, device).wait_send()
                continue

            @pl.when(c != n.c)
            def _():
                self.turn_copy(h, m, device).wait_send()

        for h in (0, 1):
            total = self.rq[4 * h].astype(F32)
            for k in (1, 2, 3):
                total = total + pltpu.roll(self.rq[4 * h + k].astype(F32), k * N, 1)
            self.fin[n.x, n.z, :, h * 128 : (h + 1) * 128] = total.astype(BF)
        ref = self.fin.at[n.x, n.z]
        for t in range(1, Z):
            self.cp.start(self.kd[t - 1], ref, ref, n.zdev(t))

    def spread(self):
        n = self.net
        for t in range(1, Z):
            self.cp.wait(self.kd[t - 1], self.fin.at[n.x, (n.z - t + Z) % Z], n.zdev(-t))
        ref = self.fin.at[n.x, pl.ds(0, SHARE)]
        for t in range(1, X):
            self.cp.start(self.ke[t - 1], ref, ref, n.xdev(t))

    def finish(self):
        n = self.net
        for t in range(1, X):
            ref = self.fin.at[(n.x - t + X) % X, pl.ds(0, SHARE)]
            self.cp.wait(self.ke[t - 1], ref, n.xdev(-t))
        for tap in range(TAPS):
            self.out[tap * N : (tap + 1) * N, :] = self.fin[tap // SHARE, tap % SHARE].astype(F32) * SCALE
        self.cp.drain()


def conv(w, e, base, s, sign, j):
    @pl.loop(0, HW // 256)
    def _(t):
        lanes = pl.ds(pl.multiple_of(t * 256, 256), 256)
        planes = e[pl.ds(base + j, 3), :, lanes].reshape(3 * C, 256)
        s[:, lanes] = jnp.dot(w[j], planes, preferred_element_type=F32)

    total = None
    for c in range(3):
        line = None
        for b in range(3):
            at = (b * 3 + c) * N
            term = shifted(s[at : at + N, :], sign * (b - 1), 0)
            line = term if line is None else line + term
        line = shifted(line, 0, sign * (c - 1))
        total = line if total is None else total + line
    return total


def grad_columns(e, c, base, a):
    for j in (0, 1):
        plane = e[base + 1 + j, pl.ds(pl.multiple_of(c * N, N), N), :].astype(F32)
        for col in range(3):
            moved = shifted(plane, 0, 1 - col)
            for row in range(3):
                at = (row * 3 + col) * N
                a[j, at : at + N, :] = shifted(moved, 1 - row, 0).astype(BF)


def grad_part(a, e, base, joined, depth, part):
    nt = (((1,), (1,)), ((), ()))
    one = lax.dot_general(a[0], e[base + depth], nt, preferred_element_type=F32)
    two = lax.dot_general(a[1], e[base + depth + 1], nt, preferred_element_type=F32)
    if depth == 2:
        one = one * joined
    if depth == 0:
        two = two * joined
    g = one + two
    for k in range(9):
        tap = depth * 9 + k
        part[tap // SHARE, pl.ds((tap % SHARE) * N, N), :] = g[k * N : (k + 1) * N].astype(BF)


def filter_rows(rows, joined, depth, at, w):
    count = rows.shape[0]
    lanes = slice(depth * C, (depth + 1) * C)
    plain = rows.astype(BF)
    masked = (rows * joined).astype(BF)
    w[0, at : at + count, lanes] = masked if depth == 2 else plain
    w[1, at : at + count, lanes] = masked if depth == 0 else plain


def backward_filter(own, joined, w):
    for a in range(3):
        filter_rows(own[(2 - a) * 288 : (3 - a) * 288, :].astype(F32), joined, a, 0, w)


def whole(
    vol, cot, own1, own2,
    output, input_grad, g1, g2,
    e1, e2, e3, e4, w1, w2, t1, t2, wf1, wf2, wb1, wb2, s, pre, a1, a2, part1, part2,
    r1, p2, r2, q, rq, fin, send, recv,
):
    net = Net()
    barrier = pltpu.get_barrier_semaphore()
    greeted = [net.in_ring(t, core) for t in range(1, Y) for core in (0, 1)]
    greeted.append(net.in_ring(0, 1 - net.core))
    total = X * Z
    for t in range(1, Z):
        greeted.append(net.zdev(t))
        greeted.append(net.dev(((net.z + t) % Z) * X + net.x, net.y + 1 - 2 * net.yl, net.core))
    for t in range(1, X):
        greeted.append(net.xdev(t))
    for t in (1, -1):
        greeted.append(net.dev((net.q + t + total) % total, net.y, net.core))
    for device in greeted:
        pl.semaphore_signal(barrier, inc=1, device_id=device, device_id_type=MESH)

    base = 2 * net.yl
    joined = jnp.where(net.dp % 16 == 0, 0.0, 1.0).astype(F32)

    def own(e):
        return pl.ds(pl.multiple_of(net.c * N, N), N)

    gathers = []
    for i, e in enumerate((e1, e2, e3, e4)):
        cp = Copies(send, recv, (i % 2) * SEMS_GATHER)
        gathers.append(Gather(net, cp, e))
        assert cp.next == (i % 2 + 1) * SEMS_GATHER
    cp = Copies(send, recv, 2 * SEMS_GATHER)
    turn1 = Turn(net, cp, w1, t1, net.x, X, net.xdev)
    cp = Copies(send, recv, cp.next)
    turn2 = Turn(net, cp, w2, t2, net.z, Z, net.zdev)
    cp = Copies(send, recv, cp.next)
    red2 = Reduce(net, cp, part2, r1.at[1], p2.at[1], r2.at[1], q.at[1], rq.at[1], fin.at[1], g2)
    cp = Copies(send, recv, cp.next)
    red1 = Reduce(net, cp, part1, r1.at[0], p2.at[0], r2.at[0], q.at[0], rq.at[0], fin.at[0], g1)
    assert cp.next <= SEMS

    for j in (0, 1):
        e1[base + 1 + j, own(e1), :] = vol[j]
        p2[j, SHARE] = jnp.zeros((2, N, 128), BF)
    for part in (part1, part2):
        part[X - 1, pl.ds((SHARE - 1) * N, N), :] = jnp.zeros((N, C), BF)
    turn1.cut(own1)
    turn2.cut(own2)
    pl.semaphore_wait(barrier, len(greeted))
    inner, outer = 1 - net.yl, net.yl
    kinds = ((inner, "inner"), (outer, "outer"))
    turn1.start()
    gathers[0].start()
    turn2.start()
    gathers[0].step(1)
    backward_filter(own2, joined, wb2)
    gathers[0].step(2)
    turn1.spread()
    backward_filter(own1, joined, wb1)
    gathers[0].step(3)
    turn2.spread()
    gathers[0].step(4)
    turn1.finish()
    turn1.filters(joined, wf1)
    gathers[0].most()
    for j, kind in kinds:
        if kind == "outer":
            gathers[0].rest()
        v = conv(wf1, e1, base, s, 1, j)
        e2[base + 1 + j, own(e2), :] = jnp.where(v > 0, v, SLOPE * v).astype(BF)
        gathers[1].start((kind,))
        pre[j] = jnp.where(v > 0, jnp.float32(1.0), jnp.float32(SLOPE))
    gathers[0].cp.drain()

    gathers[1].step(1)
    gathers[1].step(2)
    turn2.finish()
    gathers[1].step(3)
    turn2.filters(joined, wf2)
    gathers[1].step(4)
    gathers[1].most()
    for j, kind in kinds:
        if kind == "outer":
            gathers[1].rest()
        v = conv(wf2, e2, base, s, 1, j)
        slope = jnp.where(v > 0, jnp.float32(1.0), jnp.float32(SLOPE))
        e3[base + 1 + j, own(e3), :] = (cot[j].astype(F32) * slope).astype(BF)
        gathers[2].start((kind,))
        output[j] = jnp.where(v > 0, v, SLOPE * v).astype(BF)
    gathers[1].cp.drain()

    grad_columns(e3, net.c, base, a2)
    gathers[2].step(1)
    grad_part(a2, e2, base, joined, 0, part2)
    gathers[2].step(2)
    grad_part(a2, e2, base, joined, 1, part2)
    gathers[2].step(3)
    grad_part(a2, e2, base, joined, 2, part2)
    red2.start()
    gathers[2].step(4)
    gathers[2].most()
    for j, kind in kinds:
        if kind == "outer":
            gathers[2].rest()
        v = conv(wb2, e3, base, s, -1, j)
        e4[base + 1 + j, own(e4), :] = (v * pre[j]).astype(BF)
        gathers[3].start((kind,))
    gathers[2].cp.drain()

    grad_columns(e4, net.c, base, a1)
    for depth in range(3):
        grad_part(a1, e1, base, joined, depth, part1)
    red1.start()
    gathers[3].step(1)
    red2.sum_x()
    gathers[3].step(2)
    red1.sum_x()
    gathers[3].step(3)
    red2.sum_z()
    red1.sum_z()
    gathers[3].step(4)
    red1.collect()
    red2.collect()
    gathers[3].most()
    input_grad[inner] = conv(wb1, e4, base, s, -1, inner).astype(BF)
    gathers[3].rest()
    red1.spread()
    red2.spread()
    input_grad[outer] = conv(wb1, e4, base, s, -1, outer).astype(BF)
    gathers[3].cp.drain()
    red2.finish()
    red1.finish()


SEMS_GATHER = 34
SEMS = 2 * SEMS_GATHER + 10 + 14 + 2 * 36


def local(volume, filter_one, filter_two, cotangent):
    def planes(v):
        return v.transpose(0, 3, 1, 2).reshape(2, N, HW)

    def back(v):
        return v.reshape(2, N, 32, 32).transpose(0, 2, 3, 1)

    vm = pl.BlockSpec(memory_space=pltpu.VMEM)
    shape = jax.ShapeDtypeStruct
    output, input_grad, g1, g2 = pl.pallas_call(
        whole,
        out_shape=(
            shape((2, N, HW), BF),
            shape((2, N, HW), BF),
            shape((TAPS * N, C), F32),
            shape((TAPS * N, C), F32),
        ),
        in_specs=[vm] * 4,
        out_specs=[vm] * 4,
        scratch_shapes=[
            pltpu.VMEM((6, C, HW), BF),
            pltpu.VMEM((6, C, HW), BF),
            pltpu.VMEM((6, C, HW), BF),
            pltpu.VMEM((6, C, HW), BF),
            pltpu.VMEM((8, N, C), BF),
            pltpu.VMEM((8, N, 128), BF),
            pltpu.VMEM((X, C, C), BF),
            pltpu.VMEM((Z, C, 128), BF),
            pltpu.VMEM((2, 288, 3 * C), BF),
            pltpu.VMEM((2, 288, 3 * C), BF),
            pltpu.VMEM((2, 288, 3 * C), BF),
            pltpu.VMEM((2, 288, 3 * C), BF),
            pltpu.VMEM((288, HW), F32),
            pltpu.VMEM((2, N, HW), F32),
            pltpu.VMEM((2, 288, HW), BF),
            pltpu.VMEM((2, 288, HW), BF),
            pltpu.VMEM((X, SHARE * N, C), BF),
            pltpu.VMEM((X, SHARE * N, C), BF),
            pltpu.VMEM((2, X - 1, SHARE * N, C), BF),
            pltpu.VMEM((2, Z, 2, N, 128), BF),
            pltpu.VMEM((2, 2 * Z - 1, N, 128), BF),
            pltpu.VMEM((2, 128, 128), BF),
            pltpu.VMEM((2, 8, N, 128), BF),
            pltpu.VMEM((2, X, Z, N, C), BF),
            pltpu.SemaphoreType.DMA((SEMS,)),
            pltpu.SemaphoreType.DMA((SEMS,)),
        ],
        compiler_params=pltpu.CompilerParams(
            collective_id=0, has_side_effects=True, vmem_limit_bytes=50 * 1024 * 1024
        ),
    )(
        planes(volume),
        planes(cotangent),
        filter_one.reshape(TAPS * N, C),
        filter_two.reshape(TAPS * N, C),
    )
    filters = (3, 3, 3, N, C)
    return back(output), back(input_grad), g1.reshape(filters), g2.reshape(filters)


def solution(mesh):
    rows = P("dp", None, None, "chan")
    filters = P(None, None, None, "chan", None)
    return jax.shard_map(
        local,
        mesh=mesh,
        in_specs=(rows, filters, filters, rows),
        out_specs=(rows, rows, filters, filters),
        check_vma=False,
    )
```

time: 192 us -> 134 us (0.70)
  Pallas kernels: 168 us -> 126 us
  local copies, waits for them, and re-layouts: 22.5 us -> 6.38 us
    pallas_call x1, Pallas kernels: 168 us -> 126 us  [local(): pl.pallas_call(whole, out_shape=(shape((2, N, HW), BF), shape((2, N, HW),...]
    reshape x6 -> x0, local copies, waits for them, and re-layouts: 13.9 us -> none  [by_owner(): w = w.reshape(TAPS, N, 8, N).transpose(2, 1, 0, 3).reshape(8, N, TAPS * N)]
    unnamed x8 -> x6, local copies, waits for them, and re-layouts: 4 us -> 1.83 us
where the time goes in v2:
time: 134 us; the launch traced here: 133 us
  Pallas kernels  126 us (94%)
  local copies, waits for them, and re-layouts  6.38 us (5%)
    pallas_call x1, Pallas kernels, local(): pl.pallas_call(whole, out_shape=(shape((2, N, HW), BF), shape((2, N, HW),...  126 us

profile of v2, /device:TPU:1, one launch (start us, length us, event | category | flops | bytes accessed | tf_op | source)
XLA Modules:
  0.0 133.4 jit_solution(11835853464840300427)
XLA Ops:
  0.6 0.0 copy-start.1
  0.6 1.3 copy.12.vol
  1.9 0.0 copy-start
  1.9 1.3 copy.13.cot
  3.2 0.0 copy-done.1
  3.2 0.0 copy-done
  3.2 126.3 %shard_map.75 = (bf16[2,32,1024]{2,1,0:T(8,128)(2,1)S(1)}, bf16[2,32,1024]{2,1,0:T(8,128)(2,1)S(1)}, f32[864,256]{1,0:T(8,128)S(1)}, f32[864,256]{1,0:T(8,128)S(1)}) custom-call(bf16[2,32,1024]{2,1,0:T(8,128)(2,1)S(1)} %copy.12.vol, bf16[2,32,1024]{2,1,0:T(8,128)(2,1)S(1)} %copy.13.cot, bf16[864,256]{1,0:T(8,128)(2,1)S(1)} %bitcast.18, ...), custom_call_target="tpu_custom_call" | custom-call | tf_op jit(solution)/shard_map/pallas_call | solution.py:591
  129.5 1.0 copy.14
  130.5 1.0 copy.15
  131.5 0.9 copy.18
  132.5 0.9 copy.19
Async XLA Ops:
  0.6 2.6 %copy-start.1 = (bf16[3,3,3,32,256]{4,3,2,1,0:T(8,128)(2,1)S(1)}, bf16[3,3,3,32,256]{4,3,2,1,0:T(8,128)(2,1)}, u32[]{:S(2)}) copy-start(bf16[3,3,3,32,256]{4,3,2,1,0:T(8,128)(2,1)} %param.6) | copy-start | bytes 1327108
  1.9 1.3 copy-start

commit v3 on v2

--- a/solution.py
+++ b/solution.py
@@ -103,9 +103,9 @@
         self.started = []
 
 
-def block(e, slot, y, core):
+def block(e, slot, y, core, half):
     c = (y // 2) * 2 + core
-    return e.at[slot, pl.ds(pl.multiple_of(c * N, N), N), :]
+    return e.at[slot, pl.ds(pl.multiple_of(c * N + half * 16, 16), 16), :]
 
 
 class Gather:
@@ -115,23 +115,24 @@
         self.net, self.cp, self.e = net, copies, e
         self.k = {}
         s = copies.slot
-        for kind in ("outer", "inner"):
+        for kind in ("outer0", "inner0", "outer1", "inner1"):
             self.k[kind] = s()
             for d in self.BOTH:
                 for t in (1, 2, 3, 4):
-                    if t < 4 or (kind == "outer") == (d == 1):
+                    if t < 4 or (kind[:5] == "outer") == (d == 1):
                         self.k[kind, d, t] = s()
-                        if kind == "inner" or t % 2 == 0:
+                        if kind[:5] == "inner" or t % 2 == 0:
                             self.k[kind, d, t, "sib"] = s()
-                    if kind == "outer" and t % 2 == 1:
-                        self.k["far", d, t] = s()
-                        self.k["far", d, t, "sib"] = s()
+                    if kind[:5] == "outer" and t % 2 == 1:
+                        self.k["far" + kind[5], d, t] = s()
+                        self.k["far" + kind[5], d, t, "sib"] = s()
 
     def at(self, kind, d, t, core):
         y = (self.net.y - d * t + Y) % Y
-        if kind == "far":
-            return block(self.e, 5 * self.net.yl, y, core)
-        return block(self.e, 1 + 3 * (y % 2) if kind == "outer" else 2 + y % 2, y, core)
+        half = int(kind[-1])
+        if kind[:3] == "far":
+            return block(self.e, 5 * self.net.yl, y, core, half)
+        return block(self.e, 1 + 3 * (y % 2) if kind[:5] == "outer" else 2 + y % 2, y, core, half)
 
     def sibling(self):
         return self.net.in_ring(0, 1 - self.net.core)
@@ -141,7 +142,7 @@
         self.cp.start(self.k[kind, d, t], ref, ref, self.net.in_ring(d, self.net.core))
 
     def start(self, kinds=("inner", "outer")):
-        for kind in kinds:
+        for kind in [k + half for k in kinds for half in "01"]:
             for d in self.BOTH:
                 self.pass_on(kind, d, 1)
             ref = self.at(kind, 1, 0, self.net.core)
@@ -157,21 +158,23 @@
         self.cp.wait(self.k[kind, d, t], ref, n.in_ring(-d, n.core))
         if (kind, d, t + 1) in self.k:
             self.pass_on(kind, d, t + 1)
-        if kind == "outer" and t % 2 == 1:
+        if kind[:5] == "outer" and t % 2 == 1:
             q = (n.q + 1 - 2 * n.yl + X * Z) % (X * Z)
-            self.cp.start(self.k["far", d, t], ref, self.at("far", d, t, n.core), n.dev(q, n.y, n.core))
+            far = "far" + kind[5]
+            self.cp.start(self.k[far, d, t], ref, self.at(far, d, t, n.core), n.dev(q, n.y, n.core))
         if (kind, d, t, "sib") in self.k:
             self.share(kind, d, t)
 
     def far(self, t):
         n = self.net
         q = (n.q - 1 + 2 * n.yl + X * Z) % (X * Z)
-        for d in self.BOTH:
-            self.cp.wait(self.k["far", d, t], self.at("far", d, t, n.core), n.dev(q, n.y, n.core))
-            self.share("far", d, t)
+        for far in ("far0", "far1"):
+            for d in self.BOTH:
+                self.cp.wait(self.k[far, d, t], self.at(far, d, t, n.core), n.dev(q, n.y, n.core))
+                self.share(far, d, t)
 
     def step(self, t):
-        for kind in ("inner", "outer"):
+        for kind in ("inner0", "inner1", "outer0", "outer1"):
             for d in self.BOTH:
                 if (kind, d, t) in self.k:
                     self.got(kind, d, t)
@@ -180,9 +183,9 @@
 
     def most(self):
         other = 1 - self.net.core
-        for kind in ("inner", "outer"):
+        for kind in ("inner0", "inner1", "outer0", "outer1"):
             self.cp.wait(self.k[kind], self.at(kind, 1, 0, other), self.sibling())
-        self.from_sibling(("inner", "outer"))
+        self.from_sibling(("inner0", "inner1", "outer0", "outer1"))
 
     def from_sibling(self, kinds):
         for key in self.k:
@@ -190,7 +193,7 @@
                 self.cp.wait(self.k[key], self.at(*key[:3], 1 - self.net.core), self.sibling())
 
     def rest(self):
-        self.from_sibling(("far",))
+        self.from_sibling(("far0", "far1"))
 
 
 class Turn:
@@ -550,32 +553,32 @@
         gathers[3].start((kind,))
     gathers[2].cp.drain()
 
+    red2.sum_x()
     grad_columns(e4, net.c, base, a1)
     for depth in range(3):
         grad_part(a1, e1, base, joined, depth, part1)
     red1.start()
     gathers[3].step(1)
-    red2.sum_x()
     gathers[3].step(2)
+    red2.sum_z()
     red1.sum_x()
     gathers[3].step(3)
-    red2.sum_z()
+    gathers[3].step(4)
+    red2.collect()
     red1.sum_z()
-    gathers[3].step(4)
-    red1.collect()
-    red2.collect()
     gathers[3].most()
     input_grad[inner] = conv(wb1, e4, base, s, -1, inner).astype(BF)
     gathers[3].rest()
+    red2.spread()
+    red1.collect()
+    input_grad[outer] = conv(wb1, e4, base, s, -1, outer).astype(BF)
     red1.spread()
-    red2.spread()
-    input_grad[outer] = conv(wb1, e4, base, s, -1, outer).astype(BF)
+    red2.finish()
     gathers[3].cp.drain()
-    red2.finish()
     red1.finish()
 
 
-SEMS_GATHER = 34
+SEMS_GATHER = 68
 SEMS = 2 * SEMS_GATHER + 10 + 14 + 2 * 36
 
 

time: 134 us -> 126 us (0.940)
  Pallas kernels: 126 us -> 117 us
    pallas_call x1, Pallas kernels: 126 us -> 117 us  [local(): pl.pallas_call(whole, out_shape=(shape((2, N, HW), BF), shape((2, N, HW),...]
where the time goes in v3:
time: 126 us; the launch traced here: 124 us
  Pallas kernels  117 us (93%)
  local copies, waits for them, and re-layouts  6.38 us (5%)
    pallas_call x1, Pallas kernels, local(): pl.pallas_call(whole, out_shape=(shape((2, N, HW), BF), shape((2, N, HW),...  117 us
    reshape x2, local copies, waits for them, and re-layouts, planes(): return v.transpose(0, 3, 1, 2).reshape(2, N, HW)  2.54 us

profile of v3, /device:TPU:1, one launch (start us, length us, event | category | flops | bytes accessed | tf_op | source)
XLA Modules:
  0.0 124.5 jit_solution(13857047114712153994)
XLA Ops:
  0.6 0.0 copy-start.1
  0.6 1.3 %copy.12.vol = bf16[2,32,1024]{2,1,0:T(8,128)(2,1)S(1)} copy(bf16[2,32,1024]{1,2,0:T(8,128)(2,1)} %bitcast.20) | data formatting | bytes 262144 | tf_op jit(solution)/shard_map/reshape | solution.py:587
  1.9 0.0 copy-start
  1.9 1.3 %copy.13.cot = bf16[2,32,1024]{2,1,0:T(8,128)(2,1)S(1)} copy(bf16[2,32,1024]{1,2,0:T(8,128)(2,1)} %bitcast.21) | data formatting | bytes 262144 | tf_op jit(solution)/shard_map/reshape | solution.py:587
  3.2 0.0 copy-done.1
  3.2 0.0 copy-done
  3.2 117.4 %shard_map.75 = (bf16[2,32,1024]{2,1,0:T(8,128)(2,1)S(1)}, bf16[2,32,1024]{2,1,0:T(8,128)(2,1)S(1)}, f32[864,256]{1,0:T(8,128)S(1)}, f32[864,256]{1,0:T(8,128)S(1)}) custom-call(bf16[2,32,1024]{2,1,0:T(8,128)(2,1)S(1)} %copy.12.vol, bf16[2,32,1024]{2,1,0:T(8,128)(2,1)S(1)} %copy.13.cot, bf16[864,256]{1,0:T(8,128)(2,1)S(1)} %bitcast.18, ...), custom_call_target="tpu_custom_call" | custom-call | tf_op jit(solution)/shard_map/pallas_call | solution.py:594
  120.6 1.0 copy.14
  121.6 1.0 copy.15
  122.6 0.9 copy.18
  123.6 0.9 copy.19
Async XLA Ops:
  0.6 2.6 %copy-start.1 = (bf16[3,3,3,32,256]{4,3,2,1,0:T(8,128)(2,1)S(1)}, bf16[3,3,3,32,256]{4,3,2,1,0:T(8,128)(2,1)}, u32[]{:S(2)}) copy-start(bf16[3,3,3,32,256]{4,3,2,1,0:T(8,128)(2,1)} %param.6) | copy-start | bytes 1327108
  1.9 1.3 %copy-start = (bf16[3,3,3,32,256]{4,3,2,1,0:T(8,128)(2,1)S(1)}, bf16[3,3,3,32,256]{4,3,2,1,0:T(8,128)(2,1)}, u32[]{:S(2)}) copy-start(bf16[3,3,3,32,256]{4,3,2,1,0:T(8,128)(2,1)} %param.5) | copy-start | bytes 1327108
